TPU v7x, 32 devices: a whole 2x2x4 slice. The times are simulated.
32 devices in a mesh: slab: 4 (over y, core), wall: 8 (over z, x).
Axes of the slice: x: 2, y: 2, z: 4, core: 2. Of those that a mesh axis runs over, the one named last changes fastest.
Arguments:
- flow_state: float32 [64, 5, 32768], P(None, None, ('slab', 'wall')), as said below
- match_elem: int32 [262144], P(('slab', 'wall')), may hold values from 0 to 1023
- match_coord: int32 [3, 262144], P(None, ('slab', 'wall')), may hold values from 0 to 15
- match_dest: int32 [262144, 1], P(('slab', 'wall')), may hold values from 0 to 7; in each aligned block of 8192 rows (0 to 8191, 8192 to 16383, ...) at most 2560 rows name the same one
- roughness: float32 [655360], P(('slab', 'wall')), may hold values from 4 to 30
Outputs:
- rate: float32 [64, 4, 32768], P(None, None, ('slab', 'wall'))
- wall_shear: float32 [2, 655360], P(None, ('slab', 'wall'))
Inputs may be any that keep to these rules, and one draw needn't show every extreme that they name: `flow_state`: density lies between 0.8 and 1.25 and the pressure 0.4 (energy - |momentum|^2 / (2 density)) between 0.6 and 1.6 at every node. `match_dest`: among the rows of one device no wall index is named by more than 2560 rows, and in every draw some device names one wall index exactly 2560 times.
All inputs are finite; a program needn't handle non-finite values.
Results may differ from a plain program's by a relative error of at most 0.0003.
Values sent between devices are 32-bit elements; how exact they have to be, the bound alone decides.
A program may use at most 64 MiB of HBM per device.

v0:
```python
import jax
import jax.numpy as jnp
import numpy as np
from jax import lax
from jax.experimental import pallas as pl
from jax.experimental.pallas import tpu as pltpu
from jax.sharding import PartitionSpec as P

EX = 4
EY = 2
EZ = 128
ROWS = EX * EY
RES = 16
NEWTON = 8
LANES = 128
WIDTH = 512
VISCOSITY = 0.05
FOURIER_LAW_ON = 0.07 / 0.288
KARMAN = 0.41
RELAXATION = 0.35
F32 = jnp.float32
BF16 = jnp.bfloat16
PARAMS = pltpu.CompilerParams(vmem_limit_bytes=48 * 2**20)
VMEM = pl.BlockSpec(memory_space=pltpu.VMEM)
ANY = pl.BlockSpec(memory_space=pl.ANY)


def gauss_points():
    return np.array([-1.0, -1.0 / np.sqrt(5.0), 1.0 / np.sqrt(5.0), 1.0])


def derivative_matrix():
    points = gauss_points()
    weights = [
        1.0 / np.prod([points[i] - points[j] for j in range(4) if j != i]) for i in range(4)
    ]
    matrix = np.zeros((4, 4))
    for i in range(4):
        for j in range(4):
            if j != i:
                matrix[i, j] = weights[j] / weights[i] / (points[i] - points[j])
        matrix[i, i] = -np.sum(matrix[i])
    return matrix


TABLE = derivative_matrix() + np.diag([3.0, 0.0, 0.0, -3.0])


def line_slopes(values, prev_upper, next_lower):
    outs = []
    for i in range(4):
        total = None
        for j in range(4):
            coef = float(TABLE[i, j])
            if abs(coef) > 1e-12:
                term = coef * values[j]
                total = term if total is None else total + term
        if i == 0:
            total = total - 3.0 * prev_upper
        if i == 3:
            total = total + 3.0 * next_lower
        outs.append(total)
    return outs


def tile_iota(axis):
    return lax.broadcasted_iota(jnp.int32, (ROWS, EZ), axis)


def x_line(source, i, comp, edges):
    row = tile_iota(0)
    values = [source[16 * a + i, comp] for a in range(4)]
    edge = edges[i, comp % 4]
    prev_upper = jnp.where(row < EY, edge, pltpu.roll(values[3], EY, 0))
    next_lower = jnp.where(row >= ROWS - EY, edge, pltpu.roll(values[0], ROWS - EY, 0))
    return line_slopes(values, prev_upper, next_lower)


def y_line(source, i, comp):
    layer = tile_iota(0) % EY
    base = 16 * (i // 4) + i % 4
    values = [source[base + 4 * b, comp] for b in range(4)]
    prev_upper = jnp.where(layer > 0, pltpu.roll(values[3], 1, 0), values[0])
    next_lower = jnp.where(layer < EY - 1, pltpu.roll(values[0], ROWS - 1, 0), values[3])
    return values, line_slopes(values, prev_upper, next_lower)


def z_line(source, i, comp, low, high):
    lane = tile_iota(1)
    values = [source[4 * i + c, comp] for c in range(4)]
    prev_upper = jnp.where(lane == 0, low, pltpu.roll(values[3], 1, 1))
    next_lower = jnp.where(lane == EZ - 1, high, pltpu.roll(values[0], EZ - 1, 1))
    return line_slopes(values, prev_upper, next_lower)


def write_edges(source, comp_x, comp_z, edge_x, edge_z):
    edge_x[0] = source[0:16, comp_x : comp_x + 4, 0:EY, :]
    edge_x[1] = source[48:64, comp_x : comp_x + 4, ROWS - EY : ROWS, :]
    lane = tile_iota(1)

    def pack(i, carry):
        low, high = carry
        for comp in range(4):
            here = lane == 4 * i + comp
            low = jnp.where(here, source[4 * i, comp_z + comp][:, 0:1], low)
            high = jnp.where(here, source[4 * i + 3, comp_z + comp][:, EZ - 1 : EZ], high)
        return low, high

    zero = jnp.zeros((ROWS, EZ), F32)
    low, high = lax.fori_loop(0, 16, pack, (zero, zero), unroll=4)
    edge_z[0] = low
    edge_z[1] = high


def entropy_kernel(flow, ent, prim, edge_x, edge_z, held, sems):
    copies = [
        pltpu.make_async_copy(
            flow.at[:, :, pl.ds(k * EZ, EZ)], held.at[:, :, k, :], sems.at[k]
        )
        for k in range(ROWS)
    ]
    for copy in copies:
        copy.start()
    for copy in copies:
        copy.wait()

    def node(n, carry):
        rho, mx, my, mz, energy = [held[n, k] for k in range(5)]
        inv_rho = 1.0 / rho
        pressure = 0.4 * (energy - 0.5 * (mx * mx + my * my + mz * mz) * inv_rho)
        inv_p = 1.0 / pressure
        ent[n, 0] = mx * inv_p
        ent[n, 1] = my * inv_p
        ent[n, 2] = mz * inv_p
        ent[n, 3] = -rho * inv_p
        prim[n, 0] = mx * inv_rho
        prim[n, 1] = my * inv_rho
        prim[n, 2] = mz * inv_rho
        prim[n, 3] = pressure * inv_rho
        return carry

    lax.fori_loop(0, 64, node, 0, unroll=4)
    write_edges(ent, 0, 0, edge_x, edge_z)


def fill_edges(edges, low_x, high_x):
    edges[:, :, 0:EY, :] = low_x[...]
    edges[:, :, ROWS - EY : ROWS, :] = high_x[...]


def flux_kernel(ent, prim, low_x, high_x, low_z, high_z, flux, edge_x, edge_z, edges):
    fill_edges(edges, low_x, high_x)

    def lines(i, carry):
        low, high = carry
        for comp in range(4):
            for a, value in enumerate(x_line(ent, i, comp, edges)):
                flux[16 * a + i, comp] = value
            for b, value in enumerate(y_line(ent, i, comp)[1]):
                flux[16 * (i // 4) + 4 * b + i % 4, 4 + comp] = value
            outs = z_line(ent, i, comp, low[:, comp : comp + 1], high[:, comp : comp + 1])
            for c, value in enumerate(outs):
                flux[4 * i + c, 8 + comp] = value
        return pltpu.roll(low, EZ - 4, 1), pltpu.roll(high, EZ - 4, 1)

    lax.fori_loop(0, 16, lines, (low_z[...], high_z[...]))

    def node(n, carry):
        vel = [prim[n, k] for k in range(3)]
        temp = prim[n, 3]
        slope4 = [flux[n, 4 * d + 3] for d in range(3)]
        strain = [
            [temp * (flux[n, 4 * d + i] + vel[i] * slope4[d]) for i in range(3)]
            for d in range(3)
        ]
        bulk = (2.0 / 3.0 * VISCOSITY) * (strain[0][0] + strain[1][1] + strain[2][2])
        heat = FOURIER_LAW_ON * temp * temp
        tau = {}
        for d in range(3):
            for i in range(d, 3):
                entry = VISCOSITY * (strain[d][i] + strain[i][d])
                if i == d:
                    entry = entry - bulk
                tau[d, i] = tau[i, d] = entry
        for d in range(3):
            for i in range(3):
                flux[n, 4 * d + i] = tau[i, d]
            flux[n, 4 * d + 3] = (
                vel[0] * tau[0, d] + vel[1] * tau[1, d] + vel[2] * tau[2, d] + heat * slope4[d]
            )
        return carry

    lax.fori_loop(0, 64, node, 0, unroll=2)
    write_edges(flux, 0, 8, edge_x, edge_z)


def rate_kernel(flux, low_x, high_x, low_z, high_z, shear, rate, edges, held, sems):
    fill_edges(edges, low_x, high_x)

    def lines_x(i, carry):
        for comp in range(4):
            for a, value in enumerate(x_line(flux, i, comp, edges)):
                held[16 * a + i, comp] = value
        return carry

    lax.fori_loop(0, 16, lines_x, 0, unroll=2)
    row = tile_iota(0)

    def lines_y(i, carry):
        for comp in range(4):
            values, outs = y_line(flux, i, 4 + comp)
            if comp in (0, 2):
                wall = jnp.zeros((ROWS, EZ), F32)
                for ex in range(EX):
                    here = shear[comp // 2, pl.ds(EX * i + ex, 1), :]
                    wall = jnp.where(row == EY * ex, 6.0 * (values[0] - here), wall)
                outs[0] = outs[0] + wall
            for b, value in enumerate(outs):
                held[16 * (i // 4) + 4 * b + i % 4, comp] += value
        return carry

    lax.fori_loop(0, 16, lines_y, 0, unroll=2)

    def lines_z(i, carry):
        low, high = carry
        for comp in range(4):
            outs = z_line(flux, i, 8 + comp, low[:, comp : comp + 1], high[:, comp : comp + 1])
            for c, value in enumerate(outs):
                held[4 * i + c, comp] += value
        return pltpu.roll(low, EZ - 4, 1), pltpu.roll(high, EZ - 4, 1)

    lax.fori_loop(0, 16, lines_z, (low_z[...], high_z[...]), unroll=2)
    copies = [
        pltpu.make_async_copy(
            held.at[:, :, k, :], rate.at[:, :, pl.ds(k * EZ, EZ)], sems.at[k]
        )
        for k in range(ROWS)
    ]
    for copy in copies:
        copy.start()
    for copy in copies:
        copy.wait()


def two_parts(value):
    high = value.astype(BF16)
    return high, (value - high.astype(F32)).astype(BF16)


def hot(rows, index):
    ids = lax.broadcasted_iota(jnp.int32, (rows, index.shape[1]), 0)
    return jnp.where(ids == index, 1.0, 0.0).astype(BF16)


def lanes(ref, first, count):
    return jnp.concatenate([ref[pl.ds(first + j, 1), :] for j in range(count)], axis=1)


def lagrange_rows(coordinate):
    points = gauss_points()
    rows_out = []
    for i in range(4):
        product = None
        scale = 1.0
        for j in range(4):
            if j != i:
                factor = coordinate - float(points[j])
                product = factor if product is None else product * factor
                scale = scale / (points[i] - points[j])
        rows_out.append(product * float(scale))
    return rows_out


def slot_numbers(dest, wall_count, capacity):
    rows = dest.shape[0]
    masks = [jnp.where(dest == w, 1.0, 0.0) for w in range(wall_count)]
    stacked = jnp.concatenate([mask.astype(BF16) for mask in masks], axis=0)
    from_lane = lax.broadcasted_iota(jnp.int32, (LANES, 2 * LANES), 0)
    to_lane = lax.broadcasted_iota(jnp.int32, (LANES, 2 * LANES), 1)
    upper = jnp.where(from_lane < to_lane, 1.0, 0.0).astype(BF16)
    counts = jnp.dot(stacked, upper, preferred_element_type=F32)
    from_row = lax.broadcasted_iota(jnp.int32, (rows, rows), 1)
    to_row = lax.broadcasted_iota(jnp.int32, (rows, rows), 0)
    below = jnp.where(from_row < to_row, 1.0, 0.0).astype(BF16)
    rank = jnp.zeros(dest.shape, F32)
    for w in range(wall_count):
        part = counts[w * rows : (w + 1) * rows]
        earlier = jnp.dot(below, part[:, LANES:].astype(BF16), preferred_element_type=F32)
        rank = rank + masks[w] * (part[:, :LANES] + earlier)
    return dest * capacity + rank.astype(jnp.int32)


def wall_model(mass_per_volume, mom_x, mom_z, height, factor):
    vel_x = mom_x / mass_per_volume
    vel_z = mom_z / mass_per_volume
    slip_speed = jnp.maximum(jnp.sqrt(vel_x * vel_x + vel_z * vel_z), 0.5)
    reynolds = height * slip_speed * mass_per_volume / VISCOSITY
    log_term = jnp.log(factor * reynolds)
    ratio = jnp.ones_like(mass_per_volume)
    for sweep_index in range(NEWTON):
        residue = ratio - (log_term - jnp.log(ratio)) / KARMAN
        newton_slope = 1.0 + 1.0 / (KARMAN * ratio)
        ratio = ratio - RELAXATION * residue / newton_slope
    friction = slip_speed / ratio
    stress_scale = mass_per_volume * friction * friction / slip_speed
    return (stress_scale * vel_x, stress_scale * vel_z)


def wall_kernel(
    wall_count, flow, elem, coord, dest, rough, shear, outgoing,
    columns, parts, slots, probe, total, sems,
):
    copies = [
        pltpu.make_async_copy(flow.at[:, comp, :], columns.at[k], sems.at[k])
        for k, comp in enumerate((0, 1, 3))
    ]
    for copy in copies:
        copy.start()
    rows = elem.shape[0]
    grid_rows = rough.shape[0]
    elems = columns.shape[2]
    slots[...] = slot_numbers(dest[...], wall_count, grid_rows * LANES // wall_count)
    table = jnp.concatenate(two_parts(rough[...]), axis=0)
    for copy in copies:
        copy.wait()
    for k in range(3):
        high, low = two_parts(columns[k])
        parts[64 * k : 64 * k + 64] = high
        parts[192 + 64 * k : 256 + 64 * k] = low
    group = WIDTH // LANES

    def probe_block(t, carry):
        first = group * t
        element = lanes(elem, first, group)
        slot = lanes(slots, first, group)
        coords = coord[:, pl.ds(pl.multiple_of(t * WIDTH, WIDTH), WIDTH)]
        coords = (2.0 * coords.astype(F32) + 1.0) / RES - 1.0
        inner = hot(LANES, element % LANES)
        pieces = []
        for g in range(elems // LANES):
            pick = jnp.where(element // LANES == g, 1.0, 0.0).astype(BF16)
            pieces.append(inner * pick)
        element_hot = jnp.concatenate(pieces, axis=0)
        picked = jnp.dot(parts[...], element_hot, preferred_element_type=F32)
        picked = picked[:192] + picked[192:]
        basis = lagrange_rows(coords)
        along_z = jnp.concatenate([basis[c][2:3] for c in range(4)], axis=0)
        plane = jnp.concatenate([basis[b][1:2] * along_z for b in range(4)], axis=0)
        outs = []
        for k in range(3):
            mixed = basis[0][0:1] * picked[64 * k : 64 * k + 16]
            for a in range(1, 4):
                mixed = mixed + basis[a][0:1] * picked[64 * k + 16 * a : 64 * k + 16 * a + 16]
            outs.append(jnp.sum(mixed * plane, axis=0, keepdims=True))
        layer = (element // EZ % EY).astype(F32)
        outs.append(2.0 * layer + 1.0 + coords[1:2])
        found = jnp.dot(table, hot(LANES, slot % LANES), preferred_element_type=F32)
        found = found[:grid_rows] + found[grid_rows:]
        ids = lax.broadcasted_iota(jnp.int32, (grid_rows, WIDTH), 0)
        outs.append(
            jnp.sum(jnp.where(ids == slot // LANES, found, 0.0), axis=0, keepdims=True)
        )
        for k, value in enumerate(outs):
            for j in range(group):
                probe[k, pl.ds(first + j, 1), :] = value[:, LANES * j : LANES * (j + 1)]
        return carry

    lax.fori_loop(0, rows // group, probe_block, 0)
    stress = wall_model(probe[0], probe[1], probe[2], probe[3], probe[4])
    shear[0] = stress[0]
    shear[1] = stress[1]
    total[...] = jnp.zeros_like(total)

    def scatter_block(t, carry):
        first = group * t
        slot = lanes(slots, first, group)
        owner = hot(grid_rows, slot // LANES)
        left = []
        for s in range(2):
            for part in two_parts(lanes(shear.at[s], first, group)):
                left.append(owner * part)
        total[...] += lax.dot_general(
            jnp.concatenate(left, axis=0),
            hot(LANES, slot % LANES),
            (((1,), (1,)), ((), ())),
            preferred_element_type=F32,
        )
        return carry

    lax.fori_loop(0, rows // group, scatter_block, 0)
    for s in range(2):
        base = 2 * s * grid_rows
        outgoing[s] = total[base : base + grid_rows] + total[base + grid_rows : base + 2 * grid_rows]


def shape(*dims):
    return jax.ShapeDtypeStruct(dims, F32)


def exchange(edge_x, edge_z):
    outs = []
    for axis, packs in (("slab", edge_x), ("wall", edge_z)):
        count = lax.axis_size(axis)
        forward = [(i, (i + 1) % count) for i in range(count)]
        backward = [(target, source) for source, target in forward]
        outs.append(lax.ppermute(packs[1], axis, forward))
        outs.append(lax.ppermute(packs[0], axis, backward))
    return outs


def local(flow_state, match_elem, match_coord, match_dest, roughness):
    wall_count = lax.axis_size("wall")
    count = match_elem.shape[0]
    rows = count // LANES
    grid_rows = roughness.shape[0] // LANES
    elems = flow_state.shape[2]
    edge_shapes = (shape(2, 16, 4, EY, EZ), shape(2, ROWS, EZ))
    rough = lax.all_to_all(
        roughness.reshape(grid_rows, LANES), "wall", split_axis=0, concat_axis=0, tiled=True
    )
    ent, prim, edge_x, edge_z = pl.pallas_call(
        entropy_kernel,
        out_shape=(shape(64, 4, ROWS, EZ), shape(64, 4, ROWS, EZ)) + edge_shapes,
        in_specs=[ANY],
        out_specs=[VMEM] * 4,
        scratch_shapes=[pltpu.VMEM((64, 5, ROWS, EZ), F32), pltpu.SemaphoreType.DMA((ROWS,))],
        compiler_params=PARAMS,
        name="entropy_step",
    )(flow_state)
    low_x, high_x, low_z, high_z = exchange(edge_x, edge_z)
    shear, outgoing = pl.pallas_call(
        lambda *refs: wall_kernel(wall_count, *refs),
        out_shape=(shape(2, rows, LANES), shape(2, grid_rows, LANES)),
        in_specs=[ANY] + [VMEM] * 4,
        out_specs=[VMEM] * 2,
        scratch_shapes=[
            pltpu.VMEM((3, 64, elems), F32),
            pltpu.VMEM((384, elems), BF16),
            pltpu.VMEM((rows, LANES), jnp.int32),
            pltpu.VMEM((5, rows, LANES), F32),
            pltpu.VMEM((4 * grid_rows, LANES), F32),
            pltpu.SemaphoreType.DMA((3,)),
        ],
        compiler_params=PARAMS,
        cost_estimate=pl.CostEstimate(
            flops=2 * 384 * elems * count, bytes_accessed=4 * 192 * elems, transcendentals=0
        ),
        name="wall_step",
    )(
        flow_state,
        match_elem.reshape(rows, LANES),
        match_coord,
        match_dest.reshape(rows, LANES),
        rough,
    )
    wall_shear = lax.all_to_all(outgoing, "wall", split_axis=1, concat_axis=1, tiled=True)
    flux, edge_x, edge_z = pl.pallas_call(
        flux_kernel,
        out_shape=(shape(64, 12, ROWS, EZ),) + edge_shapes,
        in_specs=[VMEM] * 6,
        out_specs=[VMEM] * 3,
        scratch_shapes=[pltpu.VMEM((16, 4, ROWS, EZ), F32)],
        compiler_params=PARAMS,
        name="flux_step",
    )(ent, prim, low_x, high_x, low_z, high_z)
    low_x, high_x, low_z, high_z = exchange(edge_x, edge_z)
    rate = pl.pallas_call(
        rate_kernel,
        out_shape=shape(64, 4, elems),
        in_specs=[VMEM] * 6,
        out_specs=ANY,
        scratch_shapes=[
            pltpu.VMEM((16, 4, ROWS, EZ), F32),
            pltpu.VMEM((64, 4, ROWS, EZ), F32),
            pltpu.SemaphoreType.DMA((ROWS,)),
        ],
        compiler_params=PARAMS,
        name="rate_step",
    )(flux, low_x, high_x, low_z, high_z, shear)
    return (rate, wall_shear.reshape(2, grid_rows * LANES))


def solution(mesh):
    return jax.shard_map(
        local,
        mesh=mesh,
        in_specs=(
            P(None, None, ("slab", "wall")),
            P(("slab", "wall")),
            P(None, ("slab", "wall")),
            P(("slab", "wall"), None),
            P(("slab", "wall")),
        ),
        out_specs=(P(None, None, ("slab", "wall")), P(None, ("slab", "wall"))),
        check_vma=False,
    )
```

profile of v0, /device:TPU:0, one launch (start us, length us, event | category | flops | bytes accessed | tf_op | source)
XLA Modules:
  0.0 69.5 jit_solution(4625076736965890419)
XLA Ops:
  0.6 1.5 %all_to_all.10 = f32[8,20,128]{2,1,0:T(8,128)} reshape(f32[20480]{0:T(1024)} %param.9) | data formatting | bytes 163840 | tf_op jit(solution)/shard_map/all_to_all | solution.py:418
  2.2 7.3 %all-to-all-start = ((f32[8,20,128]{2,1,0:T(8,128)}), f32[8,20,128]{2,1,0:T(8,128)S(1)}, u32[]{:S(2)}, u32[]{:S(2)}) async-start(f32[8,20,128]{2,1,0:T(8,128)} %all_to_all.10), calls=%async_computation | async-start | bytes 196608 | tf_op jit(solution)/shard_map/all_to_all | solution.py:418
  9.4 2.1 %copy.11.flow.refs_0_ = f32[64,5,1024]{2,1,0:T(8,128)S(1)} copy(f32[64,5,1024]{2,0,1:T(8,128)} %param.5) | data formatting | bytes 2621440 | tf_op args[0]
  11.5 0.0 copy-start.2
  11.6 0.0 copy-start.3
  11.6 0.0 copy-start.4
  11.6 1.8 %entropy_step.1 = (f32[64,4,8,128]{3,2,1,0:T(8,128)S(1)}, f32[64,4,8,128]{3,2,1,0:T(8,128)S(1)}, f32[2,16,4,2,128]{4,3,2,1,0:T(2,128)S(1)}, f32[2,8,128]{2,1,0:T(8,128)S(1)}) custom-call(f32[64,5,1024]{2,1,0:T(8,128)S(1)} %copy.11.flow.refs_0_), custom_call_target="tpu_custom_call" | custom-call | tf_op jit(solution)/shard_map/entropy_step/pallas_call | solution.py:421
  13.4 0.7 %collective-permute-start.1 = (f32[16,4,2,128]{3,2,1,0:T(2,128)S(1)}, f32[16,4,2,128]{3,2,1,0:T(2,128)S(1)}, u32[]{:S(2)}, u32[]{:S(2)}) collective-permute-start(f32[16,4,2,128]{3,2,1,0:T(2,128)S(1)} %get-tuple-element.22), channel_id=1, source_target_pairs={{8,0},{16,8},{24,16},{0,24},{9,1},{17,9},{25,17},{1,25},{10,2},{18... | collective-permute-start | bytes 196616 | tf_op jit(solution)/shard_map/ppermute | solution.py:407
  14.1 0.0 collective-permute-start
  14.1 4.5 %collective-permute-start.3 = (f32[8,128]{1,0:T(8,128)S(1)}, f32[8,128]{1,0:T(8,128)S(1)}, u32[]{:S(2)}, u32[]{:S(2)}) collective-permute-start(f32[8,128]{1,0:T(8,128)S(1)} %get-tuple-element.26), channel_id=1, source_target_pairs={{1,0},{2,1},{3,2},{4,3},{5,4},{6,5},{7,6},{0,7},{9,8},{10,9},{11,1... | collective-permute-start | bytes 12296 | tf_op jit(solution)/shard_map/ppermute | solution.py:407
  18.7 0.0 collective-permute-start.2
  18.7 1.3 %collective-permute-done.3.high_z = f32[8,128]{1,0:T(8,128)S(1)} collective-permute-done((f32[8,128]{1,0:T(8,128)S(1)}, f32[8,128]{1,0:T(8,128)S(1)}, u32[]{:S(2)}, u32[]{:S(2)}) %collective-permute-start.3) | collective-permute-done | bytes 4128 | tf_op jit(solution)/shard_map/ppermute | solution.py:407
  20.0 5.0 %collective-permute-done.2.low_z = f32[8,128]{1,0:T(8,128)S(1)} collective-permute-done((f32[8,128]{1,0:T(8,128)S(1)}, f32[8,128]{1,0:T(8,128)S(1)}, u32[]{:S(2)}, u32[]{:S(2)}) %collective-permute-start.2) | collective-permute-done | bytes 4128 | tf_op jit(solution)/shard_map/ppermute | solution.py:406
  25.0 0.0 collective-permute-done.1.high_x
  25.0 0.0 collective-permute-done.low_x
  25.0 2.9 %flux_step.1 = (f32[64,12,8,128]{3,2,1,0:T(8,128)S(1)}, f32[2,16,4,2,128]{4,3,2,1,0:T(2,128)S(1)}, f32[2,8,128]{2,1,0:T(8,128)S(1)}) custom-call(f32[64,4,8,128]{3,2,1,0:T(8,128)S(1)} %get-tuple-element.11.ent, f32[64,4,8,128]{3,2,1,0:T(8,128)S(1)} %get-tuple-element.12.prim, f32[16,4,2,128]{3,2,1,0:T(2,128)S(1)} %collective-permute-done.low_x, ...), custom_call_target="tpu_custom_call" | custom-call | tf_op jit(solution)/shard_map/flux_step/pallas_call | solution.py:457
  27.9 0.0 copy-start
  27.9 1.6 %copy-done = f32[64,12,8,128]{3,2,1,0:T(8,128)} copy-done((f32[64,12,8,128]{3,2,1,0:T(8,128)}, f32[64,12,8,128]{3,2,1,0:T(8,128)S(1)}, u32[]{:S(2)}) %copy-start) | copy-done | bytes 3145752
  29.5 0.0 all-to-all-done
  29.5 0.0 copy-done.2
  29.5 0.0 copy-done.3
  29.5 0.0 copy-done.4
  29.5 18.6 %wall_step.1 = (f32[2,64,128]{2,1,0:T(8,128)S(1)}, f32[2,160,128]{2,1,0:T(8,128)S(1)}) custom-call(f32[64,5,1024]{2,1,0:T(8,128)S(1)} %copy.11.flow.refs_0_, s32[64,128]{1,0:T(8,128)S(1)} %bitcast.19, s32[3,8192]{1,0:T(4,128)S(1)} %copy-done.2, s32[64,128]{1,0:T(8,128)S(1)} %bitcast.20, f32[160,128]{1,0:T(8,128)S(1)} %all_to_all.12.refs_4_), custom_call_target="tpu_custom_call" | custom-call | flops 6442450944 | bytes 786432 | tf_op jit(solution)/shard_map/wall_step/pallas_call | solution.py:431
  48.2 0.8 %copy.13 = f32[2,160,128]{2,0,1:T(2,128)} copy(f32[2,160,128]{2,1,0:T(8,128)S(1)} %get-tuple-element.19) | data formatting | bytes 327680 | tf_op jit(solution)/shard_map/wall_step/pallas_call | solution.py:431
  49.0 3.4 %all-to-all-start.1 = ((f32[2,160,128]{2,0,1:T(2,128)}), f32[2,160,128]{2,0,1:T(2,128)S(1)}, u32[]{:S(2)}, u32[]{:S(2)}) async-start(f32[2,160,128]{2,0,1:T(2,128)} %copy.13), calls=%async_computation.1 | async-start | bytes 327680 | tf_op jit(solution)/shard_map/all_to_all | solution.py:456
  52.4 0.3 collective-permute-start.5
  52.6 0.3 collective-permute-start.4
  52.9 4.7 %collective-permute-start.7 = (f32[8,128]{1,0:T(8,128)S(1)}, f32[8,128]{1,0:T(8,128)S(1)}, u32[]{:S(2)}, u32[]{:S(2)}) collective-permute-start(f32[8,128]{1,0:T(8,128)S(1)} %get-tuple-element.24), channel_id=1, source_target_pairs={{1,0},{2,1},{3,2},{4,3},{5,4},{6,5},{7,6},{0,7},{9,8},{10,9},{11,1... | collective-permute-start | bytes 12296 | tf_op jit(solution)/shard_map/ppermute | solution.py:407
  57.6 0.0 collective-permute-start.6
  57.6 1.3 %collective-permute-done.7.high_z = f32[8,128]{1,0:T(8,128)S(1)} collective-permute-done((f32[8,128]{1,0:T(8,128)S(1)}, f32[8,128]{1,0:T(8,128)S(1)}, u32[]{:S(2)}, u32[]{:S(2)}) %collective-permute-start.7) | collective-permute-done | bytes 4128 | tf_op jit(solution)/shard_map/ppermute | solution.py:407
  58.9 5.0 %collective-permute-done.6.low_z = f32[8,128]{1,0:T(8,128)S(1)} collective-permute-done((f32[8,128]{1,0:T(8,128)S(1)}, f32[8,128]{1,0:T(8,128)S(1)}, u32[]{:S(2)}, u32[]{:S(2)}) %collective-permute-start.6) | collective-permute-done | bytes 4128 | tf_op jit(solution)/shard_map/ppermute | solution.py:406
  63.9 0.0 collective-permute-done.5.high_x
  63.9 0.0 collective-permute-done.4.low_x
  63.9 0.0 copy-start.1
  63.9 1.9 %copy-done.1 = f32[64,12,8,128]{3,2,1,0:T(8,128)S(1)} copy-done((f32[64,12,8,128]{3,2,1,0:T(8,128)S(1)}, f32[64,12,8,128]{3,2,1,0:T(8,128)}, u32[]{:S(2)}) %copy-start.1) | copy-done | bytes 3145752
  65.8 3.0 %rate_step.1 = f32[64,4,1024]{2,1,0:T(4,128)} custom-call(f32[64,12,8,128]{3,2,1,0:T(8,128)S(1)} %copy-done.1, f32[16,4,2,128]{3,2,1,0:T(2,128)S(1)} %collective-permute-done.4.low_x, f32[16,4,2,128]{3,2,1,0:T(2,128)S(1)} %collective-permute-done.5.high_x, f32[8,128]{1,0:T(8,128)S(1)} %collective-permute-done.6.low_z, ...), custom_call_target="tpu_custom_call" | custom-call | tf_op jit(solution)/shard_map/rate_step/pallas_call | solution.py:467
  68.8 0.0 all-to-all-done.1
  68.8 0.7 copy.15
  (5 shorter events, 0.0 us)
Async XLA Ops:
  2.2 27.3 %all-to-all-start = ((f32[8,20,128]{2,1,0:T(8,128)}), f32[8,20,128]{2,1,0:T(8,128)S(1)}, u32[]{:S(2)}, u32[]{:S(2)}) async-start(f32[8,20,128]{2,1,0:T(8,128)} %all_to_all.10), calls=%async_computation | async-start | bytes 196608 | tf_op jit(solution)/shard_map/all_to_all | solution.py:418
  11.5 18.0 %copy-start.2 = (s32[3,8192]{1,0:T(4,128)S(1)}, s32[3,8192]{1,0:T(4,128)}, u32[]{:S(2)}) copy-start(s32[3,8192]{1,0:T(4,128)} %refs_2_.1) | copy-start | bytes 294916
  11.6 18.0 %copy-start.3 = (s32[8192]{0:T(1024)S(1)}, s32[8192]{0:T(1024)}, u32[]{:S(2)}) copy-start(s32[8192]{0:T(1024)} %param.6) | copy-start | bytes 98308
  11.6 18.0 %copy-start.4 = (s32[8192,1]{0,1:T(1,128)S(1)}, s32[8192,1]{0,1:T(1,128)}, u32[]{:S(2)}) copy-start(s32[8192,1]{0,1:T(1,128)} %param.8) | copy-start | bytes 98308
  13.4 11.6 %collective-permute-start.1 = (f32[16,4,2,128]{3,2,1,0:T(2,128)S(1)}, f32[16,4,2,128]{3,2,1,0:T(2,128)S(1)}, u32[]{:S(2)}, u32[]{:S(2)}) collective-permute-start(f32[16,4,2,128]{3,2,1,0:T(2,128)S(1)} %get-tuple-element.22), channel_id=1, source_target_pairs={{8,0},{16,8},{24,16},{0,24},{9,1},{17,9},{25,17},{1,25},{10,2},{18... | collective-permute-start | bytes 196616 | tf_op jit(solution)/shard_map/ppermute | solution.py:407
  14.1 10.9 %collective-permute-start = (f32[16,4,2,128]{3,2,1,0:T(2,128)S(1)}, f32[16,4,2,128]{3,2,1,0:T(2,128)S(1)}, u32[]{:S(2)}, u32[]{:S(2)}) collective-permute-start(f32[16,4,2,128]{3,2,1,0:T(2,128)S(1)} %get-tuple-element.23), channel_id=1, source_target_pairs={{0,8},{8,16},{16,24},{24,0},{1,9},{9,17},{17,25},{25,1},{2,10},{10... | collective-permute-start | bytes 196616 | tf_op jit(solution)/shard_map/ppermute | solution.py:406
  14.1 5.9 %collective-permute-start.3 = (f32[8,128]{1,0:T(8,128)S(1)}, f32[8,128]{1,0:T(8,128)S(1)}, u32[]{:S(2)}, u32[]{:S(2)}) collective-permute-start(f32[8,128]{1,0:T(8,128)S(1)} %get-tuple-element.26), channel_id=1, source_target_pairs={{1,0},{2,1},{3,2},{4,3},{5,4},{6,5},{7,6},{0,7},{9,8},{10,9},{11,1... | collective-permute-start | bytes 12296 | tf_op jit(solution)/shard_map/ppermute | solution.py:407
  18.7 6.3 %collective-permute-start.2 = (f32[8,128]{1,0:T(8,128)S(1)}, f32[8,128]{1,0:T(8,128)S(1)}, u32[]{:S(2)}, u32[]{:S(2)}) collective-permute-start(f32[8,128]{1,0:T(8,128)S(1)} %get-tuple-element.27), channel_id=1, source_target_pairs={{0,1},{1,2},{2,3},{3,4},{4,5},{5,6},{6,7},{7,0},{8,9},{9,10},{10,1... | collective-permute-start | bytes 12296 | tf_op jit(solution)/shard_map/ppermute | solution.py:406
  27.9 1.6 %copy-start = (f32[64,12,8,128]{3,2,1,0:T(8,128)}, f32[64,12,8,128]{3,2,1,0:T(8,128)S(1)}, u32[]{:S(2)}) copy-start(f32[64,12,8,128]{3,2,1,0:T(8,128)S(1)} %get-tuple-element.15.flux) | copy-start | bytes 9437188
  49.0 19.9 %all-to-all-start.1 = ((f32[2,160,128]{2,0,1:T(2,128)}), f32[2,160,128]{2,0,1:T(2,128)S(1)}, u32[]{:S(2)}, u32[]{:S(2)}) async-start(f32[2,160,128]{2,0,1:T(2,128)} %copy.13), calls=%async_computation.1 | async-start | bytes 327680 | tf_op jit(solution)/shard_map/all_to_all | solution.py:456
  52.4 11.5 %collective-permute-start.5 = (f32[16,4,2,128]{3,2,1,0:T(2,128)S(1)}, f32[16,4,2,128]{3,2,1,0:T(2,128)S(1)}, u32[]{:S(2)}, u32[]{:S(2)}) collective-permute-start(f32[16,4,2,128]{3,2,1,0:T(2,128)S(1)} %get-tuple-element.20), channel_id=1, source_target_pairs={{8,0},{16,8},{24,16},{0,24},{9,1},{17,9},{25,17},{1,25},{10,2},{18... | collective-permute-start | bytes 196616 | tf_op jit(solution)/shard_map/ppermute | solution.py:407
  52.6 11.3 %collective-permute-start.4 = (f32[16,4,2,128]{3,2,1,0:T(2,128)S(1)}, f32[16,4,2,128]{3,2,1,0:T(2,128)S(1)}, u32[]{:S(2)}, u32[]{:S(2)}) collective-permute-start(f32[16,4,2,128]{3,2,1,0:T(2,128)S(1)} %get-tuple-element.21), channel_id=1, source_target_pairs={{0,8},{8,16},{16,24},{24,0},{1,9},{9,17},{17,25},{25,1},{2,10},{10... | collective-permute-start | bytes 196616 | tf_op jit(solution)/shard_map/ppermute | solution.py:406
  52.9 6.0 %collective-permute-start.7 = (f32[8,128]{1,0:T(8,128)S(1)}, f32[8,128]{1,0:T(8,128)S(1)}, u32[]{:S(2)}, u32[]{:S(2)}) collective-permute-start(f32[8,128]{1,0:T(8,128)S(1)} %get-tuple-element.24), channel_id=1, source_target_pairs={{1,0},{2,1},{3,2},{4,3},{5,4},{6,5},{7,6},{0,7},{9,8},{10,9},{11,1... | collective-permute-start | bytes 12296 | tf_op jit(solution)/shard_map/ppermute | solution.py:407
  57.6 6.3 %collective-permute-start.6 = (f32[8,128]{1,0:T(8,128)S(1)}, f32[8,128]{1,0:T(8,128)S(1)}, u32[]{:S(2)}, u32[]{:S(2)}) collective-permute-start(f32[8,128]{1,0:T(8,128)S(1)} %get-tuple-element.25), channel_id=1, source_target_pairs={{0,1},{1,2},{2,3},{3,4},{4,5},{5,6},{6,7},{7,0},{8,9},{9,10},{10,1... | collective-permute-start | bytes 12296 | tf_op jit(solution)/shard_map/ppermute | solution.py:406
  63.9 1.9 %copy-start.1 = (f32[64,12,8,128]{3,2,1,0:T(8,128)S(1)}, f32[64,12,8,128]{3,2,1,0:T(8,128)}, u32[]{:S(2)}) copy-start(f32[64,12,8,128]{3,2,1,0:T(8,128)} %copy-done) | copy-start | bytes 9437188
where the time goes:
time: 69.9 us; the launch traced here: 69.5 us
  Pallas kernels  26.3 us (38%)
  starting transfers between devices  21.1 us (30%)
  waiting for transfers between devices  12.6 us (18%)
  local copies, waits for them, and re-layouts  8.7 us (12%)
  between operations  0.77 us (1%)
    pallas_call x1, Pallas kernels, local(): pl.pallas_call(lambda *refs: wall_kernel(wall_count, *refs), out_shape=(s...  18.6 us
    ppermute x4, starting transfers between devices, exchange(): outs.append(lax.ppermute(packs[0], axis, backward))  10.2 us
    ppermute x4, waiting for transfers between devices, exchange(): outs.append(lax.ppermute(packs[1], axis, forward))  9.96 us
    all_to_all x1, starting transfers between devices, local(): lax.all_to_all(roughness.reshape(grid_rows, LANES), 'wall', split_axis=0,...  7.25 us
    unnamed x12, local copies, waits for them, and re-layouts  6.34 us
    all_to_all x1, starting transfers between devices, local(): lax.all_to_all(outgoing, 'wall', split_axis=1, concat_axis=1, tiled=True)  3.38 us
    pallas_call x1, Pallas kernels, local(): pl.pallas_call(rate_kernel, out_shape=shape(64, 4, elems), in_specs=[VMEM...  3.04 us
    pallas_call x1, Pallas kernels, local(): pl.pallas_call(flux_kernel, out_shape=(shape(64, 12, ROWS, EZ),) + edge_s...  2.87 us
  transfers between devices with their start and end apart: 10, of which 4 were waited for; matrix products, arithmetic and copies ran while one was open for 3% of the time, Pallas kernels for 11%

commit v1 on v0

--- a/solution.py
+++ b/solution.py
@@ -20,7 +20,7 @@
 RELAXATION = 0.35
 F32 = jnp.float32
 BF16 = jnp.bfloat16
-PARAMS = pltpu.CompilerParams(vmem_limit_bytes=48 * 2**20)
+MESH = pl.DeviceIdType.MESH
 VMEM = pl.BlockSpec(memory_space=pltpu.VMEM)
 ANY = pl.BlockSpec(memory_space=pl.ANY)
 
@@ -112,20 +112,9 @@
     edge_z[1] = high
 
 
-def entropy_kernel(flow, ent, prim, edge_x, edge_z, held, sems):
-    copies = [
-        pltpu.make_async_copy(
-            flow.at[:, :, pl.ds(k * EZ, EZ)], held.at[:, :, k, :], sems.at[k]
-        )
-        for k in range(ROWS)
-    ]
-    for copy in copies:
-        copy.start()
-    for copy in copies:
-        copy.wait()
-
+def entropy_step(held, ent, prim):
     def node(n, carry):
-        rho, mx, my, mz, energy = [held[n, k] for k in range(5)]
+        rho, mx, my, mz, energy = [held[k, n] for k in range(5)]
         inv_rho = 1.0 / rho
         pressure = 0.4 * (energy - 0.5 * (mx * mx + my * my + mz * mz) * inv_rho)
         inv_p = 1.0 / pressure
@@ -140,16 +129,15 @@
         return carry
 
     lax.fori_loop(0, 64, node, 0, unroll=4)
-    write_edges(ent, 0, 0, edge_x, edge_z)
-
-
-def fill_edges(edges, low_x, high_x):
-    edges[:, :, 0:EY, :] = low_x[...]
-    edges[:, :, ROWS - EY : ROWS, :] = high_x[...]
-
-
-def flux_kernel(ent, prim, low_x, high_x, low_z, high_z, flux, edge_x, edge_z, edges):
-    fill_edges(edges, low_x, high_x)
+
+
+def fill_edges(edges, near_x):
+    edges[:, :, 0:EY, :] = near_x[1]
+    edges[:, :, ROWS - EY : ROWS, :] = near_x[0]
+
+
+def flux_step(ent, prim, near_x, near_z, flux, edges):
+    fill_edges(edges, near_x)
 
     def lines(i, carry):
         low, high = carry
@@ -163,7 +151,7 @@
                 flux[4 * i + c, 8 + comp] = value
         return pltpu.roll(low, EZ - 4, 1), pltpu.roll(high, EZ - 4, 1)
 
-    lax.fori_loop(0, 16, lines, (low_z[...], high_z[...]))
+    lax.fori_loop(0, 16, lines, (near_z[1], near_z[0]))
 
     def node(n, carry):
         vel = [prim[n, k] for k in range(3)]
@@ -191,11 +179,10 @@
         return carry
 
     lax.fori_loop(0, 64, node, 0, unroll=2)
-    write_edges(flux, 0, 8, edge_x, edge_z)
-
-
-def rate_kernel(flux, low_x, high_x, low_z, high_z, shear, rate, edges, held, sems):
-    fill_edges(edges, low_x, high_x)
+
+
+def rate_step(flux, near_x, near_z, shear, edges, held):
+    fill_edges(edges, near_x)
 
     def lines_x(i, carry):
         for comp in range(4):
@@ -229,17 +216,7 @@
                 held[4 * i + c, comp] += value
         return pltpu.roll(low, EZ - 4, 1), pltpu.roll(high, EZ - 4, 1)
 
-    lax.fori_loop(0, 16, lines_z, (low_z[...], high_z[...]), unroll=2)
-    copies = [
-        pltpu.make_async_copy(
-            held.at[:, :, k, :], rate.at[:, :, pl.ds(k * EZ, EZ)], sems.at[k]
-        )
-        for k in range(ROWS)
-    ]
-    for copy in copies:
-        copy.start()
-    for copy in copies:
-        copy.wait()
+    lax.fori_loop(0, 16, lines_z, (near_z[1], near_z[0]), unroll=2)
 
 
 def two_parts(value):
@@ -306,27 +283,16 @@
     return (stress_scale * vel_x, stress_scale * vel_z)
 
 
-def wall_kernel(
-    wall_count, flow, elem, coord, dest, rough, shear, outgoing,
-    columns, parts, slots, probe, total, sems,
-):
-    copies = [
-        pltpu.make_async_copy(flow.at[:, comp, :], columns.at[k], sems.at[k])
-        for k, comp in enumerate((0, 1, 3))
-    ]
-    for copy in copies:
-        copy.start()
-    rows = elem.shape[0]
-    grid_rows = rough.shape[0]
-    elems = columns.shape[2]
-    slots[...] = slot_numbers(dest[...], wall_count, grid_rows * LANES // wall_count)
-    table = jnp.concatenate(two_parts(rough[...]), axis=0)
-    for copy in copies:
-        copy.wait()
+def split_columns(columns, parts):
     for k in range(3):
         high, low = two_parts(columns[k])
         parts[64 * k : 64 * k + 64] = high
         parts[192 + 64 * k : 256 + 64 * k] = low
+
+
+def probe_step(begin, end, elem, coord, table, slots, parts, probe):
+    elems = parts.shape[1]
+    grid_rows = table.shape[0] // 2
     group = WIDTH // LANES
 
     def probe_block(t, carry):
@@ -365,10 +331,12 @@
                 probe[k, pl.ds(first + j, 1), :] = value[:, LANES * j : LANES * (j + 1)]
         return carry
 
-    lax.fori_loop(0, rows // group, probe_block, 0)
-    stress = wall_model(probe[0], probe[1], probe[2], probe[3], probe[4])
-    shear[0] = stress[0]
-    shear[1] = stress[1]
+    lax.fori_loop(begin, end, probe_block, 0)
+
+
+def scatter_step(slots, shear, total, outgoing):
+    grid_rows = total.shape[0] // 4
+    group = WIDTH // LANES
     total[...] = jnp.zeros_like(total)
 
     def scatter_block(t, carry):
@@ -387,97 +355,209 @@
         )
         return carry
 
-    lax.fori_loop(0, rows // group, scatter_block, 0)
+    lax.fori_loop(0, slots.shape[0] // group, scatter_block, 0)
     for s in range(2):
         base = 2 * s * grid_rows
-        outgoing[s] = total[base : base + grid_rows] + total[base + grid_rows : base + 2 * grid_rows]
+        both = total[base : base + grid_rows] + total[base + grid_rows : base + 2 * grid_rows]
+        outgoing[s] = both.reshape(outgoing.shape[1:])
+
+
+def step_kernel(
+    wall_count, slab_count, flow, elem, coord, dest, rough, rate, shear_out,
+    held, columns, ent, prim, flux, rate_held, edges, edge_x, edge_z, near_x, near_z,
+    blocks, arrived, parts, slots, probe, shear, total, outgoing, landed,
+    flow_sems, rate_sems, edge_send, edge_recv, rough_send, rough_recv, shear_send, shear_recv,
+):
+    slab = lax.axis_index("slab")
+    wall = lax.axis_index("wall")
+    slab_next = lax.rem(slab + 1, slab_count)
+    slab_prev = lax.rem(slab + slab_count - 1, slab_count)
+    wall_next = lax.rem(wall + 1, wall_count)
+    wall_prev = lax.rem(wall + wall_count - 1, wall_count)
+    share = rough.shape[0] // wall_count
+    padded = blocks.shape[1]
+    flow_copies = [
+        pltpu.make_async_copy(
+            flow.at[:, :, pl.ds(k * EZ, EZ)], held.at[:, :, k, :], flow_sems.at[k]
+        )
+        for k in range(ROWS)
+    ]
+    column_copies = [
+        pltpu.make_async_copy(flow.at[comp], columns.at[k], flow_sems.at[ROWS + k])
+        for k, comp in enumerate((0, 1, 3))
+    ]
+    for copy in flow_copies + column_copies:
+        copy.start()
+    barrier = pltpu.get_barrier_semaphore()
+    peers = [{"slab": slab_next}, {"slab": slab_prev}]
+    peers += [{"wall": lax.rem(wall + d, wall_count)} for d in range(1, wall_count)]
+    for peer in peers:
+        pl.semaphore_signal(barrier, inc=1, device_id=peer, device_id_type=MESH)
+    blocks[...] = jnp.zeros_like(blocks)
+    for w in range(wall_count):
+        blocks[w, 0:share, :] = rough[w * share : (w + 1) * share, :]
+    pl.semaphore_wait(barrier, len(peers))
+
+    def remote(source, target, send, recv, peer):
+        return pltpu.make_async_remote_copy(
+            src_ref=source, dst_ref=target, send_sem=send, recv_sem=recv,
+            device_id=peer, device_id_type=MESH,
+        )
+
+    rough_copies = []
+    for d in range(1, wall_count):
+        peer = lax.rem(wall + d, wall_count)
+        rough_copies.append(
+            remote(
+                blocks.at[peer], arrived.at[wall], rough_send.at[d], rough_recv.at[d],
+                {"wall": peer},
+            )
+        )
+    for copy in rough_copies:
+        copy.start()
+    arrived[wall] = blocks[wall]
+
+    def send_edges(phase):
+        copies = []
+        for k, (buffer, near, axis, peers_of) in enumerate(
+            (
+                (edge_x, near_x, "slab", (slab_prev, slab_next)),
+                (edge_z, near_z, "wall", (wall_prev, wall_next)),
+            )
+        ):
+            for side in range(2):
+                copies.append(
+                    remote(
+                        buffer.at[phase, side], near.at[phase, side],
+                        edge_send.at[phase, 2 * k + side], edge_recv.at[phase, 2 * k + side],
+                        {axis: peers_of[side]},
+                    )
+                )
+        for copy in copies:
+            copy.start()
+        return copies
+
+    for copy in flow_copies:
+        copy.wait()
+    entropy_step(held, ent, prim)
+    write_edges(ent, 0, 0, edge_x.at[0], edge_z.at[0])
+    edge_copies = send_edges(0)
+    slots[...] = slot_numbers(dest[...], wall_count, padded * LANES)
+    for copy in column_copies:
+        copy.wait()
+    split_columns(columns, parts)
+    for copy in rough_copies:
+        copy.wait()
+    table = jnp.concatenate(two_parts(arrived[...].reshape(wall_count * padded, LANES)), axis=0)
+    steps = slots.shape[0] * LANES // WIDTH
+    first = steps // 4
+    probe_step(0, first, elem, coord, table, slots, parts, probe)
+    for copy in edge_copies:
+        copy.wait()
+    flux_step(ent, prim, near_x.at[0], near_z.at[0], flux, edges)
+    write_edges(flux, 0, 8, edge_x.at[1], edge_z.at[1])
+    edge_copies = send_edges(1)
+    probe_step(first, steps, elem, coord, table, slots, parts, probe)
+    stress = wall_model(probe[0], probe[1], probe[2], probe[3], probe[4])
+    shear[0] = stress[0]
+    shear[1] = stress[1]
+    scatter_step(slots, shear, total, outgoing)
+    shear_copies = []
+    for d in range(1, wall_count):
+        peer = lax.rem(wall + d, wall_count)
+        shear_copies.append(
+            remote(
+                outgoing.at[:, peer], landed.at[:, wall], shear_send.at[d], shear_recv.at[d],
+                {"wall": peer},
+            )
+        )
+    for copy in shear_copies:
+        copy.start()
+    for s in range(2):
+        landed[s, wall] = outgoing[s, wall]
+    for copy in edge_copies:
+        copy.wait()
+    rate_step(flux, near_x.at[1], near_z.at[1], shear, edges, rate_held)
+    rate_copies = [
+        pltpu.make_async_copy(
+            rate_held.at[:, :, k, :], rate.at[:, :, pl.ds(k * EZ, EZ)], rate_sems.at[k]
+        )
+        for k in range(ROWS)
+    ]
+    for copy in rate_copies:
+        copy.start()
+    for copy in shear_copies:
+        copy.wait()
+    for s in range(2):
+        for w in range(wall_count):
+            shear_out[w * share : (w + 1) * share, s, :] = landed[s, w, 0:share, :]
+    for copy in rate_copies:
+        copy.wait()
 
 
 def shape(*dims):
     return jax.ShapeDtypeStruct(dims, F32)
 
 
-def exchange(edge_x, edge_z):
-    outs = []
-    for axis, packs in (("slab", edge_x), ("wall", edge_z)):
-        count = lax.axis_size(axis)
-        forward = [(i, (i + 1) % count) for i in range(count)]
-        backward = [(target, source) for source, target in forward]
-        outs.append(lax.ppermute(packs[1], axis, forward))
-        outs.append(lax.ppermute(packs[0], axis, backward))
-    return outs
-
-
 def local(flow_state, match_elem, match_coord, match_dest, roughness):
     wall_count = lax.axis_size("wall")
-    count = match_elem.shape[0]
-    rows = count // LANES
+    slab_count = lax.axis_size("slab")
+    rows = match_elem.shape[0] // LANES
     grid_rows = roughness.shape[0] // LANES
+    padded = -(-(grid_rows // wall_count) // 8) * 8
     elems = flow_state.shape[2]
-    edge_shapes = (shape(2, 16, 4, EY, EZ), shape(2, ROWS, EZ))
-    rough = lax.all_to_all(
-        roughness.reshape(grid_rows, LANES), "wall", split_axis=0, concat_axis=0, tiled=True
-    )
-    ent, prim, edge_x, edge_z = pl.pallas_call(
-        entropy_kernel,
-        out_shape=(shape(64, 4, ROWS, EZ), shape(64, 4, ROWS, EZ)) + edge_shapes,
-        in_specs=[ANY],
-        out_specs=[VMEM] * 4,
-        scratch_shapes=[pltpu.VMEM((64, 5, ROWS, EZ), F32), pltpu.SemaphoreType.DMA((ROWS,))],
-        compiler_params=PARAMS,
-        name="entropy_step",
-    )(flow_state)
-    low_x, high_x, low_z, high_z = exchange(edge_x, edge_z)
-    shear, outgoing = pl.pallas_call(
-        lambda *refs: wall_kernel(wall_count, *refs),
-        out_shape=(shape(2, rows, LANES), shape(2, grid_rows, LANES)),
+    tiles = (ROWS, EZ)
+    dma = pltpu.SemaphoreType.DMA
+    rate, wall_shear = pl.pallas_call(
+        lambda *refs: step_kernel(wall_count, slab_count, *refs),
+        out_shape=(shape(64, 4, elems), shape(grid_rows, 2, LANES)),
         in_specs=[ANY] + [VMEM] * 4,
-        out_specs=[VMEM] * 2,
+        out_specs=(ANY, VMEM),
         scratch_shapes=[
+            pltpu.VMEM((5, 64) + tiles, F32),
             pltpu.VMEM((3, 64, elems), F32),
+            pltpu.VMEM((64, 4) + tiles, F32),
+            pltpu.VMEM((64, 4) + tiles, F32),
+            pltpu.VMEM((64, 12) + tiles, F32),
+            pltpu.VMEM((64, 4) + tiles, F32),
+            pltpu.VMEM((16, 4) + tiles, F32),
+            pltpu.VMEM((2, 2, 16, 4, EY, EZ), F32),
+            pltpu.VMEM((2, 2) + tiles, F32),
+            pltpu.VMEM((2, 2, 16, 4, EY, EZ), F32),
+            pltpu.VMEM((2, 2) + tiles, F32),
+            pltpu.VMEM((wall_count, padded, LANES), F32),
+            pltpu.VMEM((wall_count, padded, LANES), F32),
             pltpu.VMEM((384, elems), BF16),
             pltpu.VMEM((rows, LANES), jnp.int32),
             pltpu.VMEM((5, rows, LANES), F32),
-            pltpu.VMEM((4 * grid_rows, LANES), F32),
-            pltpu.SemaphoreType.DMA((3,)),
+            pltpu.VMEM((2, rows, LANES), F32),
+            pltpu.VMEM((4 * wall_count * padded, LANES), F32),
+            pltpu.VMEM((2, wall_count, padded, LANES), F32),
+            pltpu.VMEM((2, wall_count, padded, LANES), F32),
+            dma((ROWS + 3,)),
+            dma((ROWS,)),
+            dma((2, 4)),
+            dma((2, 4)),
+            dma((wall_count,)),
+            dma((wall_count,)),
+            dma((wall_count,)),
+            dma((wall_count,)),
         ],
-        compiler_params=PARAMS,
+        compiler_params=pltpu.CompilerParams(
+            vmem_limit_bytes=48 * 2**20, collective_id=0, has_side_effects=True
+        ),
         cost_estimate=pl.CostEstimate(
-            flops=2 * 384 * elems * count, bytes_accessed=4 * 192 * elems, transcendentals=0
+            flops=2 * 384 * elems * rows * LANES, bytes_accessed=4 * 576 * elems, transcendentals=0
         ),
-        name="wall_step",
+        name="residual_step",
     )(
-        flow_state,
+        flow_state.transpose(1, 0, 2),
         match_elem.reshape(rows, LANES),
         match_coord,
         match_dest.reshape(rows, LANES),
-        rough,
+        roughness.reshape(grid_rows, LANES),
     )
-    wall_shear = lax.all_to_all(outgoing, "wall", split_axis=1, concat_axis=1, tiled=True)
-    flux, edge_x, edge_z = pl.pallas_call(
-        flux_kernel,
-        out_shape=(shape(64, 12, ROWS, EZ),) + edge_shapes,
-        in_specs=[VMEM] * 6,
-        out_specs=[VMEM] * 3,
-        scratch_shapes=[pltpu.VMEM((16, 4, ROWS, EZ), F32)],
-        compiler_params=PARAMS,
-        name="flux_step",
-    )(ent, prim, low_x, high_x, low_z, high_z)
-    low_x, high_x, low_z, high_z = exchange(edge_x, edge_z)
-    rate = pl.pallas_call(
-        rate_kernel,
-        out_shape=shape(64, 4, elems),
-        in_specs=[VMEM] * 6,
-        out_specs=ANY,
-        scratch_shapes=[
-            pltpu.VMEM((16, 4, ROWS, EZ), F32),
-            pltpu.VMEM((64, 4, ROWS, EZ), F32),
-            pltpu.SemaphoreType.DMA((ROWS,)),
-        ],
-        compiler_params=PARAMS,
-        name="rate_step",
-    )(flux, low_x, high_x, low_z, high_z, shear)
-    return (rate, wall_shear.reshape(2, grid_rows * LANES))
+    return (rate, wall_shear.transpose(1, 0, 2).reshape(2, grid_rows * LANES))
 
 
 def solution(mesh):

time: 69.9 us -> 45 us (0.64)
  starting transfers between devices: 21.1 us -> 0 us
  waiting for transfers between devices: 12.6 us -> 0 us
  Pallas kernels: 26.3 us -> 37.8 us
  local copies, waits for them, and re-layouts: 8.7 us -> 6.25 us
    ppermute x8 -> x0, waiting for transfers between devices: 12.6 us -> none  [the longest x4 9.96 us: exchange(): outs.append(lax.ppermute(packs[1], axis, forward))]
    pallas_call x4 -> x1, Pallas kernels: 26.3 us -> 37.8 us  [local(): pl.pallas_call(lambda *refs: step_kernel(wall_count, slab_count, *refs),...]
    all_to_all x2 -> x0, starting transfers between devices: 10.6 us -> none  [the longest x1 7.25 us: local(): lax.all_to_all(roughness.reshape(grid_rows, LANES), 'wall', split_axis=0,...]
    ppermute x8 -> x0, starting transfers between devices: 10.5 us -> none  [the longest x4 10.2 us: exchange(): outs.append(lax.ppermute(packs[0], axis, backward))]
    all_to_all x2 -> x0, local copies, waits for them, and re-layouts: 1.54 us -> none  [local(): lax.all_to_all(roughness.reshape(grid_rows, LANES), 'wall', split_axis=0,...]
    pallas_call x1 -> x0, local copies, waits for them, and re-layouts: 0.79 us -> none  [local(): pl.pallas_call(lambda *refs: wall_kernel(wall_count, *refs), out_shape=(s...]
  transfers between devices with their start and end apart: 10 -> 0, of which waited for: 4 -> 0; matrix products, arithmetic and copies ran while one was open for 3% -> 0% of each run, Pallas kernels for 11% -> 0%
where the time goes in v1:
time: 45 us; the launch traced here: 44.7 us
  Pallas kernels  37.8 us (84%)
  local copies, waits for them, and re-layouts  6.25 us (14%)
  between operations  0.65 us (1%)
    pallas_call x1, Pallas kernels, local(): pl.pallas_call(lambda *refs: step_kernel(wall_count, slab_count, *refs),...  37.8 us
    unnamed x12, local copies, waits for them, and re-layouts  6.25 us

profile of v1, /device:TPU:0, one launch (start us, length us, event | category | flops | bytes accessed | tf_op | source)
XLA Modules:
  0.0 44.7 jit_solution(7972769152065943809)
XLA Ops:
  0.6 0.0 copy-start
  0.6 1.3 %copy-done = f32[64,5,1024]{2,0,1:T(8,128)S(1)} copy-done((f32[64,5,1024]{2,0,1:T(8,128)S(1)}, f32[64,5,1024]{2,0,1:T(8,128)}, u32[]{:S(2)}) %copy-start) | copy-done | bytes 1310744
  1.9 0.0 copy-start.1
  2.0 0.9 %copy-done.1 = s32[3,8192]{1,0:T(4,128)S(1)} copy-done((s32[3,8192]{1,0:T(4,128)S(1)}, s32[3,8192]{1,0:T(4,128)}, u32[]{:S(2)}) %copy-start.1) | copy-done | bytes 98328
  2.9 0.0 copy-start.2
  2.9 0.9 %copy-done.2 = f32[20480]{0:T(1024)S(1)} copy-done((f32[20480]{0:T(1024)S(1)}, f32[20480]{0:T(1024)}, u32[]{:S(2)}) %copy-start.2) | copy-done | bytes 81944
  3.7 0.0 copy-start.3
  3.7 0.8 %copy-done.3 = s32[8192]{0:T(1024)S(1)} copy-done((s32[8192]{0:T(1024)S(1)}, s32[8192]{0:T(1024)}, u32[]{:S(2)}) %copy-start.3) | copy-done | bytes 32792
  4.5 0.0 copy-start.4
  4.5 0.8 %copy-done.4 = s32[8192,1]{0,1:T(1,128)S(1)} copy-done((s32[8192,1]{0,1:T(1,128)S(1)}, s32[8192,1]{0,1:T(1,128)}, u32[]{:S(2)}) %copy-start.4) | copy-done | bytes 32792
  5.3 37.8 %residual_step.1 = (f32[64,4,1024]{2,1,0:T(4,128)S(1)}, f32[160,2,128]{2,1,0:T(2,128)S(1)}) custom-call(f32[5,64,1024]{2,1,0:T(8,128)S(1)} %bitcast.8, s32[64,128]{1,0:T(8,128)S(1)} %bitcast.10, s32[3,8192]{1,0:T(4,128)S(1)} %copy-done.1, s32[64,128]{1,0:T(8,128)S(1)} %bitcast.11, f32[160,128]{1,0:T(8,128)S(1)} %bitcast.9), custom_call_target="tpu_custom_call" | custom-call | flops 6442450944 | bytes 2359296 | tf_op jit(solution)/shard_map/residual_step/pallas_call | solution.py:511
  43.1 1.0 %copy.9 = f32[64,4,1024]{2,1,0:T(4,128)} copy(f32[64,4,1024]{2,1,0:T(4,128)S(1)} %get-tuple-element.8) | data formatting | bytes 2097152
  44.0 0.7 %copy.10 = f32[2,20480]{1,0:T(2,128)} copy(f32[2,20480]{1,0:T(2,128)S(1)} %bitcast.7) | data formatting | bytes 327680
Async XLA Ops:
  0.6 1.3 %copy-start = (f32[64,5,1024]{2,0,1:T(8,128)S(1)}, f32[64,5,1024]{2,0,1:T(8,128)}, u32[]{:S(2)}) copy-start(f32[64,5,1024]{2,0,1:T(8,128)} %param.5) | copy-start | bytes 3932164
  1.9 0.9 %copy-start.1 = (s32[3,8192]{1,0:T(4,128)S(1)}, s32[3,8192]{1,0:T(4,128)}, u32[]{:S(2)}) copy-start(s32[3,8192]{1,0:T(4,128)} %refs_2_.1) | copy-start | bytes 294916
  2.9 0.9 %copy-start.2 = (f32[20480]{0:T(1024)S(1)}, f32[20480]{0:T(1024)}, u32[]{:S(2)}) copy-start(f32[20480]{0:T(1024)} %param.9) | copy-start | bytes 245764
  3.7 0.8 %copy-start.3 = (s32[8192]{0:T(1024)S(1)}, s32[8192]{0:T(1024)}, u32[]{:S(2)}) copy-start(s32[8192]{0:T(1024)} %param.6) | copy-start | bytes 98308
  4.5 0.8 %copy-start.4 = (s32[8192,1]{0,1:T(1,128)S(1)}, s32[8192,1]{0,1:T(1,128)}, u32[]{:S(2)}) copy-start(s32[8192,1]{0,1:T(1,128)} %param.8) | copy-start | bytes 98308

commit v2 on v1

--- a/solution.py
+++ b/solution.py
@@ -13,7 +13,7 @@
 RES = 16
 NEWTON = 8
 LANES = 128
-WIDTH = 512
+WIDTH = 2048
 VISCOSITY = 0.05
 FOURIER_LAW_ON = 0.07 / 0.288
 KARMAN = 0.41
@@ -23,6 +23,7 @@
 MESH = pl.DeviceIdType.MESH
 VMEM = pl.BlockSpec(memory_space=pltpu.VMEM)
 ANY = pl.BlockSpec(memory_space=pl.ANY)
+HBM = pl.BlockSpec(memory_space=pltpu.HBM)
 
 
 def gauss_points():
@@ -290,15 +291,13 @@
         parts[192 + 64 * k : 256 + 64 * k] = low
 
 
-def probe_step(begin, end, elem, coord, table, slots, parts, probe):
+def probe_step(begin, end, elem, coord, parts, probe):
     elems = parts.shape[1]
-    grid_rows = table.shape[0] // 2
     group = WIDTH // LANES
 
     def probe_block(t, carry):
         first = group * t
         element = lanes(elem, first, group)
-        slot = lanes(slots, first, group)
         coords = coord[:, pl.ds(pl.multiple_of(t * WIDTH, WIDTH), WIDTH)]
         coords = (2.0 * coords.astype(F32) + 1.0) / RES - 1.0
         inner = hot(LANES, element % LANES)
@@ -320,18 +319,30 @@
             outs.append(jnp.sum(mixed * plane, axis=0, keepdims=True))
         layer = (element // EZ % EY).astype(F32)
         outs.append(2.0 * layer + 1.0 + coords[1:2])
-        found = jnp.dot(table, hot(LANES, slot % LANES), preferred_element_type=F32)
-        found = found[:grid_rows] + found[grid_rows:]
-        ids = lax.broadcasted_iota(jnp.int32, (grid_rows, WIDTH), 0)
-        outs.append(
-            jnp.sum(jnp.where(ids == slot // LANES, found, 0.0), axis=0, keepdims=True)
-        )
         for k, value in enumerate(outs):
             for j in range(group):
                 probe[k, pl.ds(first + j, 1), :] = value[:, LANES * j : LANES * (j + 1)]
         return carry
 
     lax.fori_loop(begin, end, probe_block, 0)
+
+
+def gather_step(table, slots, probe):
+    grid_rows = table.shape[0] // 2
+    group = WIDTH // LANES
+
+    def gather_block(t, carry):
+        first = group * t
+        slot = lanes(slots, first, group)
+        found = jnp.dot(table, hot(LANES, slot % LANES), preferred_element_type=F32)
+        found = found[:grid_rows] + found[grid_rows:]
+        ids = lax.broadcasted_iota(jnp.int32, (grid_rows, WIDTH), 0)
+        value = jnp.sum(jnp.where(ids == slot // LANES, found, 0.0), axis=0, keepdims=True)
+        for j in range(group):
+            probe[4, pl.ds(first + j, 1), :] = value[:, LANES * j : LANES * (j + 1)]
+        return carry
+
+    lax.fori_loop(0, slots.shape[0] // group, gather_block, 0)
 
 
 def scatter_step(slots, shear, total, outgoing):
@@ -363,7 +374,8 @@
 
 
 def step_kernel(
-    wall_count, slab_count, flow, elem, coord, dest, rough, rate, shear_out,
+    wall_count, slab_count, flow, elem_in, coord_in, dest_in, rough_in, rate, shear_out,
+    elem, coord, dest, rough,
     held, columns, ent, prim, flux, rate_held, edges, edge_x, edge_z, near_x, near_z,
     blocks, arrived, parts, slots, probe, shear, total, outgoing, landed,
     flow_sems, rate_sems, edge_send, edge_recv, rough_send, rough_recv, shear_send, shear_recv,
@@ -386,7 +398,13 @@
         pltpu.make_async_copy(flow.at[comp], columns.at[k], flow_sems.at[ROWS + k])
         for k, comp in enumerate((0, 1, 3))
     ]
-    for copy in flow_copies + column_copies:
+    small_copies = [
+        pltpu.make_async_copy(source, target, flow_sems.at[ROWS + 3 + k])
+        for k, (source, target) in enumerate(
+            ((rough_in, rough), (dest_in, dest), (elem_in, elem), (coord_in, coord))
+        )
+    ]
+    for copy in small_copies[:1] + flow_copies + small_copies[1:] + column_copies:
         copy.start()
     barrier = pltpu.get_barrier_semaphore()
     peers = [{"slab": slab_next}, {"slab": slab_prev}]
@@ -394,6 +412,7 @@
     for peer in peers:
         pl.semaphore_signal(barrier, inc=1, device_id=peer, device_id_type=MESH)
     blocks[...] = jnp.zeros_like(blocks)
+    small_copies[0].wait()
     for w in range(wall_count):
         blocks[w, 0:share, :] = rough[w * share : (w + 1) * share, :]
     pl.semaphore_wait(barrier, len(peers))
@@ -442,22 +461,25 @@
     entropy_step(held, ent, prim)
     write_edges(ent, 0, 0, edge_x.at[0], edge_z.at[0])
     edge_copies = send_edges(0)
+    for copy in small_copies[1:]:
+        copy.wait()
     slots[...] = slot_numbers(dest[...], wall_count, padded * LANES)
     for copy in column_copies:
         copy.wait()
     split_columns(columns, parts)
-    for copy in rough_copies:
-        copy.wait()
-    table = jnp.concatenate(two_parts(arrived[...].reshape(wall_count * padded, LANES)), axis=0)
     steps = slots.shape[0] * LANES // WIDTH
     first = steps // 4
-    probe_step(0, first, elem, coord, table, slots, parts, probe)
+    probe_step(0, first, elem, coord, parts, probe)
     for copy in edge_copies:
         copy.wait()
     flux_step(ent, prim, near_x.at[0], near_z.at[0], flux, edges)
     write_edges(flux, 0, 8, edge_x.at[1], edge_z.at[1])
     edge_copies = send_edges(1)
-    probe_step(first, steps, elem, coord, table, slots, parts, probe)
+    probe_step(first, steps, elem, coord, parts, probe)
+    for copy in rough_copies:
+        copy.wait()
+    table = jnp.concatenate(two_parts(arrived[...].reshape(wall_count * padded, LANES)), axis=0)
+    gather_step(table, slots, probe)
     stress = wall_model(probe[0], probe[1], probe[2], probe[3], probe[4])
     shear[0] = stress[0]
     shear[1] = stress[1]
@@ -511,9 +533,13 @@
     rate, wall_shear = pl.pallas_call(
         lambda *refs: step_kernel(wall_count, slab_count, *refs),
         out_shape=(shape(64, 4, elems), shape(grid_rows, 2, LANES)),
-        in_specs=[ANY] + [VMEM] * 4,
+        in_specs=[ANY] + [HBM] * 4,
         out_specs=(ANY, VMEM),
         scratch_shapes=[
+            pltpu.VMEM((rows, LANES), jnp.int32),
+            pltpu.VMEM(match_coord.shape, jnp.int32),
+            pltpu.VMEM((rows, LANES), jnp.int32),
+            pltpu.VMEM((grid_rows, LANES), F32),
             pltpu.VMEM((5, 64) + tiles, F32),
             pltpu.VMEM((3, 64, elems), F32),
             pltpu.VMEM((64, 4) + tiles, F32),
@@ -534,7 +560,7 @@
             pltpu.VMEM((4 * wall_count * padded, LANES), F32),
             pltpu.VMEM((2, wall_count, padded, LANES), F32),
             pltpu.VMEM((2, wall_count, padded, LANES), F32),
-            dma((ROWS + 3,)),
+            dma((ROWS + 7,)),
             dma((ROWS,)),
             dma((2, 4)),
             dma((2, 4)),

time: 45 us -> 39.7 us (0.88)
  Pallas kernels: 37.8 us -> 32.4 us
    pallas_call x1, Pallas kernels: 37.8 us -> 32.4 us  [local(): pl.pallas_call(lambda *refs: step_kernel(wall_count, slab_count, *refs),...]
where the time goes in v2:
time: 39.7 us; the launch traced here: 39.3 us
  Pallas kernels  32.4 us (82%)
  local copies, waits for them, and re-layouts  6.25 us (16%)
  between operations  0.65 us (2%)
    pallas_call x1, Pallas kernels, local(): pl.pallas_call(lambda *refs: step_kernel(wall_count, slab_count, *refs),...  32.4 us
    unnamed x12, local copies, waits for them, and re-layouts  6.25 us

profile of v2, /device:TPU:0, one launch (start us, length us, event | category | flops | bytes accessed | tf_op | source)
XLA Modules:
  0.0 39.3 jit_solution(15417181407766617097)
XLA Ops:
  0.6 0.0 copy-start
  0.6 1.3 %copy-done = f32[64,5,1024]{2,0,1:T(8,128)S(1)} copy-done((f32[64,5,1024]{2,0,1:T(8,128)S(1)}, f32[64,5,1024]{2,0,1:T(8,128)}, u32[]{:S(2)}) %copy-start) | copy-done | bytes 1310744
  1.9 0.0 copy-start.1
  2.0 0.9 %copy-done.1 = s32[3,8192]{1,0:T(4,128)S(1)} copy-done((s32[3,8192]{1,0:T(4,128)S(1)}, s32[3,8192]{1,0:T(4,128)}, u32[]{:S(2)}) %copy-start.1) | copy-done | bytes 98328
  2.9 0.0 copy-start.2
  2.9 0.9 %copy-done.2 = f32[20480]{0:T(1024)S(1)} copy-done((f32[20480]{0:T(1024)S(1)}, f32[20480]{0:T(1024)}, u32[]{:S(2)}) %copy-start.2) | copy-done | bytes 81944
  3.7 0.0 copy-start.3
  3.7 0.8 %copy-done.3 = s32[8192]{0:T(1024)S(1)} copy-done((s32[8192]{0:T(1024)S(1)}, s32[8192]{0:T(1024)}, u32[]{:S(2)}) %copy-start.3) | copy-done | bytes 32792
  4.5 0.0 copy-start.4
  4.5 0.8 %copy-done.4 = s32[8192,1]{0,1:T(1,128)S(1)} copy-done((s32[8192,1]{0,1:T(1,128)S(1)}, s32[8192,1]{0,1:T(1,128)}, u32[]{:S(2)}) %copy-start.4) | copy-done | bytes 32792
  5.3 32.4 %residual_step.1 = (f32[64,4,1024]{2,1,0:T(4,128)S(1)}, f32[160,2,128]{2,1,0:T(2,128)S(1)}) custom-call(f32[5,64,1024]{2,1,0:T(8,128)S(1)} %bitcast.8, s32[64,128]{1,0:T(8,128)S(1)} %bitcast.10, s32[3,8192]{1,0:T(4,128)S(1)} %copy-done.1, s32[64,128]{1,0:T(8,128)S(1)} %bitcast.11, f32[160,128]{1,0:T(8,128)S(1)} %bitcast.9), custom_call_target="tpu_custom_call" | custom-call | flops 6442450944 | bytes 2359296 | tf_op jit(solution)/shard_map/residual_step/pallas_call | solution.py:533
  37.7 1.0 %copy.9 = f32[64,4,1024]{2,1,0:T(4,128)} copy(f32[64,4,1024]{2,1,0:T(4,128)S(1)} %get-tuple-element.8) | data formatting | bytes 2097152
  38.7 0.7 %copy.10 = f32[2,20480]{1,0:T(2,128)} copy(f32[2,20480]{1,0:T(2,128)S(1)} %bitcast.7) | data formatting | bytes 327680
Async XLA Ops:
  0.6 1.3 %copy-start = (f32[64,5,1024]{2,0,1:T(8,128)S(1)}, f32[64,5,1024]{2,0,1:T(8,128)}, u32[]{:S(2)}) copy-start(f32[64,5,1024]{2,0,1:T(8,128)} %param.5) | copy-start | bytes 3932164
  1.9 0.9 %copy-start.1 = (s32[3,8192]{1,0:T(4,128)S(1)}, s32[3,8192]{1,0:T(4,128)}, u32[]{:S(2)}) copy-start(s32[3,8192]{1,0:T(4,128)} %refs_2_.1) | copy-start | bytes 294916
  2.9 0.9 %copy-start.2 = (f32[20480]{0:T(1024)S(1)}, f32[20480]{0:T(1024)}, u32[]{:S(2)}) copy-start(f32[20480]{0:T(1024)} %param.9) | copy-start | bytes 245764
  3.7 0.8 %copy-start.3 = (s32[8192]{0:T(1024)S(1)}, s32[8192]{0:T(1024)}, u32[]{:S(2)}) copy-start(s32[8192]{0:T(1024)} %param.6) | copy-start | bytes 98308
  4.5 0.8 %copy-start.4 = (s32[8192,1]{0,1:T(1,128)S(1)}, s32[8192,1]{0,1:T(1,128)}, u32[]{:S(2)}) copy-start(s32[8192,1]{0,1:T(1,128)} %param.8) | copy-start | bytes 98308

commit v3 on v2

--- a/solution.py
+++ b/solution.py
@@ -570,7 +570,7 @@
             dma((wall_count,)),
         ],
         compiler_params=pltpu.CompilerParams(
-            vmem_limit_bytes=48 * 2**20, collective_id=0, has_side_effects=True
+            vmem_limit_bytes=60 * 2**20, collective_id=0, has_side_effects=True
         ),
         cost_estimate=pl.CostEstimate(
             flops=2 * 384 * elems * rows * LANES, bytes_accessed=4 * 576 * elems, transcendentals=0

time: 39.7 us -> 35.7 us (0.90)
  local copies, waits for them, and re-layouts: 6.25 us -> 2.97 us
  Pallas kernels: 32.4 us -> 31.9 us
    unnamed x12 -> x4, local copies, waits for them, and re-layouts: 6.25 us -> 2.97 us
    pallas_call x1, Pallas kernels: 32.4 us -> 31.9 us  [local(): pl.pallas_call(lambda *refs: step_kernel(wall_count, slab_count, *refs),...]
where the time goes in v3:
time: 35.7 us; the launch traced here: 35.5 us
  Pallas kernels  31.9 us (89%)
  local copies, waits for them, and re-layouts  2.97 us (8%)
  between operations  0.65 us (2%)
    pallas_call x1, Pallas kernels, local(): pl.pallas_call(lambda *refs: step_kernel(wall_count, slab_count, *refs),...  31.9 us
    unnamed x4, local copies, waits for them, and re-layouts  2.97 us

profile of v3, /device:TPU:0, one launch (start us, length us, event | category | flops | bytes accessed | tf_op | source)
XLA Modules:
  0.0 35.5 jit_solution(13658304395227712148)
XLA Ops:
  0.6 31.9 %residual_step.1 = (f32[64,4,1024]{2,1,0:T(4,128)}, f32[160,2,128]{2,1,0:T(2,128)}) custom-call(f32[5,64,1024]{2,1,0:T(8,128)} %bitcast.8, s32[64,128]{1,0:T(8,128)} %bitcast.10, s32[3,8192]{1,0:T(4,128)} %refs_2_.1, s32[64,128]{1,0:T(8,128)} %bitcast.11, f32[160,128]{1,0:T(8,128)} %bitcast.9), custom_call_target="tpu_custom_call" | custom-call | flops 6442450944 | bytes 2359296 | tf_op jit(solution)/shard_map/residual_step/pallas_call | solution.py:533
  32.5 0.0 copy-start
  32.5 2.3 %copy.9 = f32[64,4,1024]{2,1,0:T(4,128)} copy(f32[64,4,1024]{2,1,0:T(4,128)} %get-tuple-element.8) | data formatting | bytes 2097152
  34.8 0.0 copy-done
  34.8 0.7 %copy.10 = f32[2,20480]{1,0:T(2,128)} copy(f32[2,20480]{1,0:T(2,128)S(1)} %bitcast.7) | data formatting | bytes 327680
Async XLA Ops:
  32.5 2.3 %copy-start = (f32[160,2,128]{2,1,0:T(2,128)S(1)}, f32[160,2,128]{2,1,0:T(2,128)}, u32[]{:S(2)}) copy-start(f32[160,2,128]{2,1,0:T(2,128)} %get-tuple-element.5) | copy-start | bytes 491524
